TPU v7x, 128 devices: a whole 4x4x4 slice. The times are simulated.
128 devices in a mesh: patch: 32 (over y, z, core), coarse: 4 (over x).
Axes of the slice: x: 4, y: 4, z: 4, core: 2. Of those that a mesh axis runs over, the one named last changes fastest.
Arguments:
- residual: bfloat16 [2, 2, 196608, 256], P(None, None, ('patch', 'coarse')), may hold values from -6 to 6
- patch_inv: bfloat16 [512, 2, 1024, 1024], P(('patch', 'coarse')), may hold values from -0.1875 to 0.1875
- coarse_basis: bfloat16 [512, 2, 1024, 32], P(('patch', 'coarse')), may hold values from -0.1875 to 0.1875
- coarse_inv: bfloat16 [64, 2, 32, 32], P('coarse'), may hold values from -1 to 1
- patch_slots: int32 [512, 512], P(('patch', 'coarse')), may hold values from 0 to 1791, as said below
- send_rows: int32 [128, 2, 128], P(('patch', 'coarse')), may hold values from 0 to 1535, as said below
- coarse_block: int32 [512], P(('patch', 'coarse')), may hold values from 0 to 63
Outputs:
- correction: bfloat16 [2, 2, 196608, 256], P(None, None, ('patch', 'coarse'))
Inputs may be any that keep to these rules, and one draw needn't show every extreme that they name: `send_rows`: within each of the two blocks of a device the 128 rows are distinct. `patch_slots`: the 512 positions of a patch are distinct; they hold its device's rows (p mod 4) * 384 to (p mod 4 + 1) * 384 - 1, 64 positions of 1536 or more, and other rows of its device below 1536; each position of 1536 or more is used by exactly one patch of the device.
All inputs are finite; a program needn't handle non-finite values.
Results may differ from a plain program's by a relative error of at most 0.006.
Values may be sent and summed in bfloat16 or wider, within the bound.
A program may use at most 128 MiB of HBM per device.

v0:
```python
import jax
import jax.numpy as jnp
from jax import lax
from jax.sharding import PartitionSpec as P


def passed_along(value, axis, steps):
    count = lax.axis_size(axis)
    pairs = [(source, (source + steps) % count) for source in range(count)]
    return lax.ppermute(value, axis, pairs)


def spread_rows(selector, terms, form):
    upper_part = terms.astype(jnp.bfloat16)
    lower_part = (terms - upper_part.astype(jnp.float32)).astype(jnp.bfloat16)
    first = jnp.einsum(form, selector, upper_part, preferred_element_type=jnp.float32)
    return first + jnp.einsum(form, selector, lower_part, preferred_element_type=jnp.float32)


def per_device(residual, patch_inv, coarse_basis, coarse_inv, patch_slots, send_rows, coarse_block):
    wave_count = residual.shape[0]
    node_rows = residual.shape[2]
    patches = patch_inv.shape[0]
    patch_nodes = patch_inv.shape[2] // 2
    coarse_width = coarse_basis.shape[3]
    slot_rows = send_rows.shape[2]
    ext_rows = node_rows + 2 * slot_rows
    blocks_all = coarse_inv.shape[0] * lax.axis_size("coarse")
    highest = lax.Precision.HIGHEST
    node_ids = jnp.arange(node_rows, dtype=jnp.int32)
    up_select = (send_rows[0, 0][:, None] == node_ids[None, :]).astype(jnp.bfloat16)
    down_select = (send_rows[0, 1][:, None] == node_ids[None, :]).astype(jnp.bfloat16)
    upward = jnp.einsum(
        "kn,wqnr->wqkr", up_select, residual, preferred_element_type=jnp.float32
    ).astype(jnp.bfloat16)
    downward = jnp.einsum(
        "kn,wqnr->wqkr", down_select, residual, preferred_element_type=jnp.float32
    ).astype(jnp.bfloat16)
    from_below = passed_along(upward, ("patch", "coarse"), 1)
    from_above = passed_along(downward, ("patch", "coarse"), -1)
    extended = jnp.concatenate([residual, from_below, from_above], axis=2)
    ext_select = (
        patch_slots[:, :, None] == jnp.arange(ext_rows, dtype=jnp.int32)[None, None, :]
    ).astype(jnp.bfloat16)
    gathered = jnp.einsum(
        "pne,wqer->wqpnr", ext_select, extended, preferred_element_type=jnp.float32
    ).astype(jnp.bfloat16)
    basis_cols = coarse_basis.reshape(patches, wave_count, 2, patch_nodes, coarse_width)
    restricted = jnp.einsum(
        "pwqnc,wqpnr->pwcr", basis_cols, gathered, preferred_element_type=jnp.float32
    )
    member = coarse_block[:, None] == jnp.arange(blocks_all, dtype=jnp.int32)[None, :]
    partial_sums = jnp.einsum(
        "pb,pwcr->bwcr", member.astype(jnp.float32), restricted, precision=highest
    )
    totals = lax.psum(partial_sums, ("patch", "coarse"))
    inverses = lax.all_gather(coarse_inv, "coarse", axis=0, tiled=True)
    coarse_coef = jnp.einsum(
        "bwcd,bwdr->bwcr", inverses.astype(jnp.float32), totals, precision=highest
    ).astype(jnp.bfloat16)
    patch_coef = jnp.einsum(
        "pb,bwcr->pwcr",
        member.astype(jnp.bfloat16),
        coarse_coef,
        preferred_element_type=jnp.float32,
    ).astype(jnp.bfloat16)
    inverse = patch_inv.reshape(patches, wave_count, 2, patch_nodes, 2, patch_nodes)
    local_terms = jnp.einsum(
        "pwabqn,wqpnr->wapbr", inverse, gathered, preferred_element_type=jnp.float32
    )
    local_terms = local_terms + jnp.einsum(
        "pwqnc,pwcr->wqpnr", basis_cols, patch_coef, preferred_element_type=jnp.float32
    )
    collected = spread_rows(ext_select, local_terms, "pne,wqpnr->wqer")
    to_lower = collected[:, :, node_rows : node_rows + slot_rows]
    to_upper = collected[:, :, node_rows + slot_rows :]
    back_from_above = passed_along(to_lower.astype(jnp.bfloat16), ("patch", "coarse"), -1).astype(
        to_lower.dtype
    )
    back_from_below = passed_along(to_upper.astype(jnp.bfloat16), ("patch", "coarse"), 1).astype(
        to_upper.dtype
    )
    summed = collected[:, :, :node_rows]
    summed = summed + spread_rows(up_select, back_from_above, "kn,wqkr->wqnr")
    summed = summed + spread_rows(down_select, back_from_below, "kn,wqkr->wqnr")
    return summed.astype(jnp.bfloat16)


def solution(mesh):
    placed = (
        P(None, None, ("patch", "coarse"), None),
        P(("patch", "coarse"), None, None, None),
        P(("patch", "coarse"), None, None, None),
        P("coarse", None, None, None),
        P(("patch", "coarse"), None),
        P(("patch", "coarse"), None, None),
        P(("patch", "coarse")),
    )
    return jax.shard_map(
        per_device,
        mesh=mesh,
        in_specs=placed,
        out_specs=P(None, None, ("patch", "coarse"), None),
        check_vma=False,
    )
```

profile of v0, /device:TPU:0, one launch (start us, length us, event | category | flops | bytes accessed | tf_op | source)
XLA Modules:
  0.0 274.4 jit_solution(16813826966453386580)
XLA Ops:
  6.5 0.0 copy-start
  6.5 0.0 all-reduce.2.cloned.1.call-start
  6.5 0.8 slice_bitcast_fusion.1
  7.4 2.6 fusion.39
  10.0 1.6 collective-permute-start
  11.7 3.2 %fusion.40 = bf16[2,2,128,256]{3,2,1,0:T(8,128)(2,1)} fusion(bf16[2,2,1536,256]{3,2,1,0:T(8,128)(2,1)} %param.7, s32[128]{0:T(128)S(1)} %get-tuple-element.8), kind=kOutput, calls=%fused_computation.38 | convolution fusion | flops 402980864 | bytes 3408384 | tf_op jit(solution)/shard_map/kn,wqnr->wqkr/dot_general | solution.py:36
  14.9 0.0 copy-start.5
  14.9 6.6 %collective-permute-start.1 = (bf16[2,2,128,256]{3,2,1,0:T(8,128)(2,1)}, bf16[2,2,128,256]{3,2,1,0:T(8,128)(2,1)}, u32[]{:S(2)}, u32[]{:S(2)}) collective-permute-start(bf16[2,2,128,256]{3,2,1,0:T(8,128)(2,1)} %fusion.40), channel_id=1, source_target_pairs={{0,127},{1,0},{2,1},{3,2},{4,3},{5,4},{6,5},{7,6},{8,7},{9,8},{10,... | collective-permute-start | bytes 786440 | tf_op jit(solution)/shard_map/ppermute | solution.py:10
  21.5 0.0 copy-done
  21.5 2.8 %copy.22 = bf16[2,2,1536,256]{2,3,1,0:T(8,128)(2,1)} copy(bf16[2,2,1536,256]{3,2,1,0:T(8,128)(2,1)S(1)} %copy-done) | data formatting | bytes 6291456 | tf_op args[0]
  24.3 0.1 collective-permute-done
  24.4 1.1 copy.23
  25.6 0.2 collective-permute-done.1
  25.8 1.1 copy.24
  26.9 0.0 copy-done.5
  26.9 0.0 copy-start.2
  26.9 10.3 %fusion.29 = bf16[2,2,256,4,512]{4,2,3,1,0:T(8,128)(2,1)S(1)} fusion(s32[4,512]{1,0:T(4,128)S(1)} %copy-done.5, bf16[2,2,128,256]{2,3,1,0:T(8,128)(2,1)S(1)} %copy.24, bf16[2,2,128,256]{2,3,1,0:T(8,128)(2,1)S(1)} %copy.23, bf16[2,2,1536,256]{2,3,1,0:T(8,128)(2,1)} %copy.22), kind=kOutput, calls=%fused_computation.30 | convolution fusion | flops 7532969984 | bytes 7872512 | tf_op jit(solution)/shard_map/pne,wqer->wqpnr/dot_general | solution.py:45
  37.2 0.0 copy-start.6
  37.2 0.0 copy-start.4
  37.2 2.0 copy-done.6
  39.3 0.0 copy-done.2
  39.3 1.3 fusion.36
  40.6 0.0 copy-done.4
  40.6 3.9 %fusion.68 = f32[64,2,32,256]{3,0,2,1:T(8,128)} fusion(f32[4,2,32,256]{3,2,1,0:T(8,128)S(1)} %fusion.36, s32[4]{0:T(128)S(1)} %copy-done.4), kind=kOutput, calls=%fused_computation.60 | convolution fusion | flops 50331904 | bytes 4456464 | tf_op jit(solution)/shard_map/pb,pwcr->bwcr/dot_general | solution.py:53
  44.5 0.0 all-reduce.2.cloned.1.call-update
  44.5 0.4 reshape.11
  44.9 0.0 copy-start.3
  44.9 28.0 %reshape.10 = bf16[4,2,2,512,2,512]{5,4,3,2,1,0:T(2,128)(2,1)} reshape(bf16[4,2,1024,1024]{3,2,1,0:T(8,128)(2,1)} %param.8) | data formatting | bytes 33554432 | tf_op jit(solution)/shard_map/reshape | solution.py:67
  72.9 0.0 copy-done.3
  72.9 14.8 %all_gather.3 = bf16[64,2,32,32]{3,2,1,0:T(8,128)(2,1)S(1)} all-gather(bf16[16,2,32,32]{3,2,1,0:T(8,128)(2,1)S(1)} %copy-done.3), channel_id=1, replica_groups=mesh['patch'=32,'coarse'=4] {'coarse'}, dimensions={0}, use_global_device_ids=true | all-gather | bytes 327680 | tf_op jit(solution)/shard_map/all_gather | solution.py:57
  87.6 15.0 %fusion = f32[2,4,256,2,512,1]{4,2,5,3,1,0:T(8,128)} fusion(bf16[4,2,2,512,2,512]{5,4,3,2,1,0:T(2,128)(2,1)} %reshape.10, bf16[2,2,256,4,512]{4,2,3,1,0:T(8,128)(2,1)} %copy-done.6), kind=kOutput, calls=%fused_computation | convolution fusion | flops 4294967296 | bytes 29360128 | tf_op jit(solution)/shard_map/pwabqn,wqpnr->wapbr/dot_general | solution.py:68
  102.7 97.4 %all-reduce.2.cloned.1.call-done = f32[64,2,32,256]{3,0,2,1:T(8,128)} async-done(((f32[64,2,32,256]{3,0,2,1:T(8,128)}), f32[64,2,32,256]{3,0,2,1:T(8,128)}) %all-reduce.2.cloned.1.call-update) | async-done | bytes 4194320 | tf_op jit(solution)/shard_map/psum | solution.py:56
  200.0 7.1 %convert_bitcast_fusion = bf16[64,2,32,256]{3,2,1,0:T(8,128)(2,1)S(1)} fusion(bf16[64,2,32,32]{3,2,1,0:T(8,128)(2,1)S(1)} %all_gather.3, f32[64,2,32,256]{3,0,2,1:T(8,128)} %all-reduce.2.cloned.1.call-done), kind=kOutput, calls=%fused_computation.33 | convolution fusion | flops 403701760 | bytes 6553600 | tf_op jit(solution)/shard_map/bwcd,bwdr->bwcr/dot_general | solution.py:58
  207.2 1.2 fusion.44
  208.4 1.3 fusion.60
  209.7 0.0 copy-start.1
  209.7 3.2 %copy-done.1 = f32[2,4,256,2,512]{4,2,3,1,0:T(8,128)} copy-done((f32[2,4,256,2,512]{4,2,3,1,0:T(8,128)}, f32[2,4,256,2,512]{4,2,3,1,0:T(8,128)S(1)}, u32[]{:S(2)}) %copy-start.1) | copy-done | bytes 8388632
  212.9 13.1 %fusion.4 = f32[2,2,256,1792,1]{3,2,1,4,0:T(8,128)} fusion(s32[4,512]{1,0:T(4,128)S(1)} %copy-done.5, f32[2,4,256,2,512]{4,2,3,1,0:T(8,128)S(1)} %fusion.60, f32[2,4,256,2,512,1]{4,2,5,3,1,0:T(8,128)} %fusion), kind=kOutput, calls=%fused_computation.5 | convolution fusion | flops 7530348544 | bytes 24125440 | tf_op jit(solution)/shard_map/pne,wqpnr->wqer/dot_general | solution.py:17
  226.0 18.2 %fusion.78 = (bf16[2,2,1792,256]{2,3,1,0:T(8,128)(2,1)S(1)}, f32[2,2,1792,256]{2,3,1,0:T(8,128)}) fusion(f32[2,2,256,1792,1]{3,2,1,4,0:T(8,128)} %fusion.4, s32[4,512]{1,0:T(4,128)S(1)} %copy-done.5, f32[2,4,256,2,512]{4,2,3,1,0:T(8,128)} %copy-done.1, f32[2,4,256,2,512,1]{4,2,5,3,1,0:T(8,128)} %fusion), kind=kOutput, calls=%fused_computation.71 | convolution fusion | flops 7527727104 | bytes 35135488 | tf_op jit(solution)/shard_map/pne,wqpnr->wqer/dot_general | solution.py:16
  244.2 0.1 fusion.77
  244.3 4.0 %collective-permute-start.2 = (bf16[2,2,128,256]{2,3,1,0:T(8,128)(2,1)S(1)}, bf16[2,2,128,256]{2,3,1,0:T(8,128)(2,1)S(1)}, u32[]{:S(2)}, u32[]{:S(2)}) collective-permute-start(bf16[2,2,128,256]{2,3,1,0:T(8,128)(2,1)S(1)} %get-tuple-element.5), channel_id=1, source_target_pairs={{0,127},{1,0},{2,1},{3,2},{4,3},{5,4},{6,5},{7,6},{8,7},{9,8},{10,... | collective-permute-start | bytes 786440 | tf_op jit(solution)/shard_map/ppermute | solution.py:10
  248.3 0.0 collective-permute-start.3
  248.3 4.1 %collective-permute-done.2 = bf16[2,2,128,256]{2,3,1,0:T(8,128)(2,1)S(1)} collective-permute-done((bf16[2,2,128,256]{2,3,1,0:T(8,128)(2,1)S(1)}, bf16[2,2,128,256]{2,3,1,0:T(8,128)(2,1)S(1)}, u32[]{:S(2)}, u32[]{:S(2)}) %collective-permute-start.2) | collective-permute-done | bytes 262176 | tf_op jit(solution)/shard_map/ppermute | solution.py:10
  252.4 1.1 fusion.48
  253.5 1.1 fusion.50
  254.6 4.9 %collective-permute-done.3 = bf16[2,2,128,256]{2,3,1,0:T(8,128)(2,1)S(1)} collective-permute-done((bf16[2,2,128,256]{2,3,1,0:T(8,128)(2,1)S(1)}, bf16[2,2,128,256]{2,3,1,0:T(8,128)(2,1)S(1)}, u32[]{:S(2)}, u32[]{:S(2)}) %collective-permute-start.3) | collective-permute-done | bytes 262176 | tf_op jit(solution)/shard_map/ppermute | solution.py:10
  259.5 1.1 fusion.54
  260.6 4.2 %fusion.16 = bf16[2,2,1536,256]{2,3,1,0:T(8,128)(2,1)S(1)} fusion(f32[2,2,1792,256]{2,3,1,0:T(8,128)} %get-tuple-element.10, f32[2,2,256,1536]{3,2,1,0:T(8,128)S(1)} %fusion.54, f32[2,2,256,1536]{3,2,1,0:T(8,128)S(1)} %fusion.50, f32[2,2,256,1536]{3,2,1,0:T(8,128)S(1)} %fusion.48, bf16[2,2,128,256]{2,3,1,0:T(8,128)(2,1)S(1)} %collective-permute-done.3, ...), kind=kOutput, calls=%fused_computation.19 | convolution fusion | flops 410714112 | bytes 28574208 | tf_op jit(solution)/shard_map/kn,wqkr->wqnr/dot_general | solution.py:16
  264.8 2.8 %copy.36 = bf16[2,2,1536,256]{3,2,1,0:T(8,128)(2,1)} copy(bf16[2,2,1536,256]{2,3,1,0:T(8,128)(2,1)S(1)} %fusion.16) | data formatting | bytes 6291456 | tf_op jit(solution)/shard_map/convert_element_type | solution.py:86
Async XLA Ops:
  6.5 15.0 %copy-start = (bf16[2,2,1536,256]{3,2,1,0:T(8,128)(2,1)S(1)}, bf16[2,2,1536,256]{3,2,1,0:T(8,128)(2,1)}, u32[]{:S(2)}) copy-start(bf16[2,2,1536,256]{3,2,1,0:T(8,128)(2,1)} %param.7) | copy-start | bytes 9437188
  6.5 193.5 %all-reduce.2.cloned.1.call-start = ((), (), s32[]{:S(2)}) async-start(), calls=%async_computation | async-start | bytes 8388608 | tf_op jit(solution)/shard_map/psum | solution.py:56
  10.0 14.4 %collective-permute-start = (bf16[2,2,128,256]{3,2,1,0:T(8,128)(2,1)S(1)}, bf16[2,2,128,256]{3,2,1,0:T(8,128)(2,1)}, u32[]{:S(2)}, u32[]{:S(2)}) collective-permute-start(bf16[2,2,128,256]{3,2,1,0:T(8,128)(2,1)S(1)} %fusion.39), channel_id=1, source_target_pairs={{0,1},{1,2},{2,3},{3,4},{4,5},{5,6},{6,7},{7,8},{8,9},{9,10},{10,1... | collective-permute-start | bytes 786440 | tf_op jit(solution)/shard_map/ppermute | solution.py:10
  14.9 12.0 %copy-start.5 = (s32[4,512]{1,0:T(4,128)S(1)}, s32[4,512]{1,0:T(4,128)}, u32[]{:S(2)}) copy-start(s32[4,512]{1,0:T(4,128)} %param.11) | copy-start | bytes 24580
  14.9 10.9 %collective-permute-start.1 = (bf16[2,2,128,256]{3,2,1,0:T(8,128)(2,1)}, bf16[2,2,128,256]{3,2,1,0:T(8,128)(2,1)}, u32[]{:S(2)}, u32[]{:S(2)}) collective-permute-start(bf16[2,2,128,256]{3,2,1,0:T(8,128)(2,1)} %fusion.40), channel_id=1, source_target_pairs={{0,127},{1,0},{2,1},{3,2},{4,3},{5,4},{6,5},{7,6},{8,7},{9,8},{10,... | collective-permute-start | bytes 786440 | tf_op jit(solution)/shard_map/ppermute | solution.py:10
  26.9 12.4 %copy-start.2 = (bf16[4,2,1024,32]{2,3,1,0:T(8,128)(2,1)S(1)}, bf16[4,2,1024,32]{2,3,1,0:T(8,128)(2,1)}, u32[]{:S(2)}) copy-start(bf16[4,2,1024,32]{2,3,1,0:T(8,128)(2,1)} %param.9) | copy-start | bytes 1572868
  37.2 2.1 copy-start.6
  37.2 3.4 %copy-start.4 = (s32[4]{0:T(128)S(1)}, s32[4]{0:T(128)}, u32[]{:S(2)}) copy-start(s32[4]{0:T(128)} %param.13) | copy-start | bytes 52
  44.9 28.0 %copy-start.3 = (bf16[16,2,32,32]{3,2,1,0:T(8,128)(2,1)S(1)}, bf16[16,2,32,32]{3,2,1,0:T(8,128)(2,1)}, u32[]{:S(2)}) copy-start(bf16[16,2,32,32]{3,2,1,0:T(8,128)(2,1)} %param.10) | copy-start | bytes 196612
  209.7 3.2 %copy-start.1 = (f32[2,4,256,2,512]{4,2,3,1,0:T(8,128)}, f32[2,4,256,2,512]{4,2,3,1,0:T(8,128)S(1)}, u32[]{:S(2)}) copy-start(f32[2,4,256,2,512]{4,2,3,1,0:T(8,128)S(1)} %fusion.60) | copy-start | bytes 25165828
  244.3 8.1 %collective-permute-start.2 = (bf16[2,2,128,256]{2,3,1,0:T(8,128)(2,1)S(1)}, bf16[2,2,128,256]{2,3,1,0:T(8,128)(2,1)S(1)}, u32[]{:S(2)}, u32[]{:S(2)}) collective-permute-start(bf16[2,2,128,256]{2,3,1,0:T(8,128)(2,1)S(1)} %get-tuple-element.5), channel_id=1, source_target_pairs={{0,127},{1,0},{2,1},{3,2},{4,3},{5,4},{6,5},{7,6},{8,7},{9,8},{10,... | collective-permute-start | bytes 786440 | tf_op jit(solution)/shard_map/ppermute | solution.py:10
  248.3 11.2 %collective-permute-start.3 = (bf16[2,2,128,256]{2,3,1,0:T(8,128)(2,1)S(1)}, bf16[2,2,128,256]{2,3,1,0:T(8,128)(2,1)S(1)}, u32[]{:S(2)}, u32[]{:S(2)}) collective-permute-start(bf16[2,2,128,256]{2,3,1,0:T(8,128)(2,1)S(1)} %get-tuple-element.6), channel_id=1, source_target_pairs={{0,1},{1,2},{2,3},{3,4},{4,5},{5,6},{6,7},{7,8},{8,9},{9,10},{10,1... | collective-permute-start | bytes 786440 | tf_op jit(solution)/shard_map/ppermute | solution.py:10
Sparse Core Ops, SparseCore 0:
  44.6 155.3 all-reduce.1
where the time goes:
time: 275 us; the launch traced here: 274 us
  waiting for transfers between devices  107 us (39%)
  matrix products  84.7 us (31%)
  local copies, waits for them, and re-layouts  42.4 us (15%)
  blocking collectives  14.8 us (5%)
  between operations  13.5 us (5%)
  starting transfers between devices  12.3 us (4%)
    psum x1, waiting for transfers between devices, per_device(): totals = lax.psum(partial_sums, ('patch', 'coarse'))  97.4 us
    reshape x1, local copies, waits for them, and re-layouts, per_device(): patch_inv.reshape(patches, wave_count, 2, patch_nodes, 2, patch_nodes)  28 us
    dot_general x3, matrix products, spread_rows(): jnp.einsum(form, selector, upper_part, preferred_element_type=jnp.float32)  23.4 us
    dot_general x3, matrix products, spread_rows(): jnp.einsum(form, selector, lower_part, preferred_element_type=jnp.float32)  15.3 us
    dot_general x1, matrix products, per_device(): jnp.einsum('pwabqn,wqpnr->wapbr', inverse, gathered, preferred_element_ty...  15 us
    all_gather x1, blocking collectives, per_device(): inverses = lax.all_gather(coarse_inv, 'coarse', axis=0, tiled=True)  14.8 us
    ppermute x4, starting transfers between devices, passed_along(): return lax.ppermute(value, axis, pairs)  12.3 us
    dot_general x1, matrix products, per_device(): jnp.einsum('pne,wqer->wqpnr', ext_select, extended, preferred_element_typ...  10.3 us
  transfers between devices with their start and end apart: 5, of which 5 were waited for; matrix products, arithmetic and copies ran while one was open for 19% of the time, Pallas kernels for 0%

commit v1 on v0

v1 whole, which is shorter than its diff:
```python
import functools

import jax
import jax.numpy as jnp
from jax import lax
from jax.experimental import pallas as pl
from jax.experimental.pallas import tpu as pltpu
from jax.sharding import PartitionSpec as P

MESH = pl.DeviceIdType.MESH
F32 = jnp.float32
BF16 = jnp.bfloat16
NODE = 1536
CORE = 384
PN = 512
XS = 4
GM = 8
HALF = 1024


def dot(a, b):
    return lax.dot_general(a, b, (((1,), (0,)), ((), ())), preferred_element_type=F32)


def dot_t(a, b):
    return lax.dot_general(a, b, (((1,), (1,)), ((), ())), preferred_element_type=F32)


def iota(shape, axis):
    return lax.broadcasted_iota(jnp.int32, shape, axis).astype(F32)


def hot(mask):
    return jnp.where(mask, 1.0, 0.0).astype(BF16)


def columns(row):
    return jnp.transpose(jnp.broadcast_to(row, (128, 128)))


def kernel(
    groups,
    res_hbm, inv_hbm, basis_hbm, cinv_hbm, slots_ref, send_ref, cb_ref,
    out_ref,
    res_v, inv_v, basis_v, cinv_v, ci_v,
    krow_s, ss, sst, sel_o, sel_ot, sel_r, sel_rt, perm, permt,
    hs1, hr1, hs2, hr2, u, gath, bt, bp, cbig, own, yor, yo, yr,
    cbt, cbr, oh, oht, sb1, xb, db, s2, cgs, cg, rb, cf,
    load_sem, inv_sem, hs_sem, hr_sem, hs2_sem, hr2_sem,
    cb_ss, cb_rs, ci_ss, ci_rs, a_ss, a_rs, b_ss, b_rs, c_ss, c_rs, d_ss, d_rs,
):
    pidx = lax.axis_index("patch")
    x = lax.axis_index("coarse")
    g = pidx // 2
    h = pidx % 2
    m = h * XS + x
    me = pidx * XS + x
    count = groups * GM
    per_owner = 32 // groups
    orow = per_owner * 32

    def at_member(mm):
        return (g * 2 + mm // XS, mm % XS)

    def at_group(gg):
        return (gg * 2 + h, x)

    def at_device(d):
        return (d // XS, d % XS)

    upper = at_device((me + 1) % count)
    lower = at_device((me + count - 1) % count)

    def remote(src, dst, ssem, rsem, dev):
        return pltpu.make_async_remote_copy(
            src_ref=src, dst_ref=dst, send_sem=ssem, recv_sem=rsem,
            device_id=dev, device_id_type=MESH,
        )

    loads = [
        pltpu.make_async_copy(res_hbm.at[i // 2, i % 2], res_v.at[i], load_sem.at[i])
        for i in range(4)
    ]
    loads.append(pltpu.make_async_copy(basis_hbm, basis_v, load_sem.at[4]))
    loads.append(pltpu.make_async_copy(cinv_hbm, cinv_v, load_sem.at[5]))
    for copy in loads:
        copy.start()

    def inv_copy(i):
        return pltpu.make_async_copy(inv_hbm.at[i // 2, i % 2], inv_v.at[i], inv_sem.at[i])

    for i in range(8):
        inv_copy(i).start()

    barrier = pltpu.get_barrier_semaphore()
    peers = [upper, lower]
    peers += [at_member((m + k) % GM) for k in range(1, GM)]
    peers += [at_group((g + k) % groups) for k in range(1, groups)]
    for dev in peers:
        pl.semaphore_signal(barrier, inc=1, device_id=dev, device_id_type=MESH)

    for b in range(2):
        row = send_ref[0, b : b + 1, :].astype(F32)
        col = columns(row)
        for t in range(NODE // 128):
            ss[128 * b : 128 * b + 128, 128 * t : 128 * t + 128] = hot(
                col == iota((128, 128), 1) + float(128 * t)
            )
        sst[:, 128 * b : 128 * b + 128] = hot(iota((NODE, 128), 0) == row)

    lane = lax.broadcasted_iota(jnp.int32, (8, 128), 1)
    target = jnp.where(
        lane < 64,
        jnp.where(lane < 32, cb_ref[0], cb_ref[1]),
        jnp.where(lane < 96, cb_ref[2], cb_ref[3]),
    ) * 32 + lane % 32
    cbt[...] = target.astype(F32)
    cbr[0] = target.astype(F32)

    def halo_out(w4, b):
        return remote(
            hs1.at[w4, pl.ds(128 * b, 128)], hr1.at[w4, pl.ds(128 * b, 128)],
            hs_sem.at[w4, b], hr_sem.at[w4, b], upper if b == 0 else lower,
        )

    for w4 in range(4):
        loads[w4].wait()
        hs1[w4] = dot(ss[...], res_v[w4]).astype(BF16)
        if w4 == 0:
            pl.semaphore_wait(barrier, len(peers))
        for b in range(2):
            halo_out(w4, b).start()

    def cb_out(k):
        return remote(cbt, cbr.at[k], cb_ss.at[k], cb_rs.at[k], at_member((m + k) % GM))

    for k in range(1, GM):
        cb_out(k).start()
    loads[5].wait()
    first = 32 * h + per_owner * g
    holder = first // 16
    mine = cinv_v.at[pl.ds(first % 16, per_owner)]

    def ci_out(k):
        return remote(mine, ci_v, ci_ss.at[k], ci_rs, (pidx, (x + k) % XS))

    @pl.when(x == holder)
    def _():
        for k in range(1, XS):
            ci_out(k).start()
        ci_v[...] = cinv_v[pl.ds(first % 16, per_owner)]

    s = slots_ref[...].astype(F32)
    base = iota((4, PN), 0) * float(CORE)
    is_rem = s >= float(NODE)
    is_core = (s >= base) & (s < base + float(CORE))
    weight = jnp.where(is_rem, 256.0, jnp.where(is_core, 0.0, 1.0)).astype(BF16)
    tri = hot(iota((PN, PN), 0) < iota((PN, PN), 1))
    ranks = dot(weight, tri)
    rank_r = jnp.floor(ranks * (1.0 / 256.0))
    rank_o = ranks - 256.0 * rank_r
    place = jnp.where(is_core, s - base, jnp.where(is_rem, 448.0 + rank_r, 384.0 + rank_o))
    for p in range(4):
        krow_s[p] = place[p : p + 1, :]

    def build(p, carry):
        krow = krow_s[p]
        permt[p] = hot(iota((PN, PN), 0) == krow)
        for c in range(4):
            col = columns(krow[:, 128 * c : 128 * c + 128])
            for t in range(4):
                perm[p, 128 * c : 128 * c + 128, 128 * t : 128 * t + 128] = hot(
                    col == iota((128, 128), 1) + float(128 * t)
                )
        return carry

    lax.fori_loop(0, 4, build, 0)
    s_hi = jnp.floor(s * (1.0 / 128.0))
    s_lo = s - 128.0 * s_hi
    s_hi, s_lo = s_hi.astype(BF16), s_lo.astype(BF16)
    values = []
    for p in range(4):
        tail = perm[p, :, 384:512]
        values.append((128.0 * dot(s_hi, tail) + dot(s_lo, tail))[p : p + 1, :])
    low_lane = lax.broadcasted_iota(jnp.int32, (1, 128), 1) < 64
    for j in range(2):
        v0, v1 = values[2 * j], values[2 * j + 1]
        row_o = jnp.where(low_lane, v0, pltpu.roll(v1, 64, 1))
        row_r = jnp.where(low_lane, pltpu.roll(v0, 64, 1), v1) - float(NODE)
        here = slice(128 * j, 128 * j + 128)
        col = columns(row_o)
        for t in range(NODE // 128):
            sel_o[here, 128 * t : 128 * t + 128] = hot(
                col == iota((128, 128), 1) + float(128 * t)
            )
        sel_ot[:, here] = hot(iota((NODE, 128), 0) == row_o)
        col = columns(row_r)
        for t in range(2):
            sel_r[here, 128 * t : 128 * t + 128] = hot(
                col == iota((128, 128), 1) + float(128 * t)
            )
        sel_rt[:, here] = hot(iota((256, 128), 0) == row_r)

    for w4 in range(4):
        others = dot(sel_o[...], res_v[w4]).astype(BF16)
        for p in range(4):
            u[p, w4, 0:CORE] = res_v[w4, CORE * p : CORE * p + CORE]
            u[p, w4, CORE : CORE + 64] = others[64 * p : 64 * p + 64]

    loads[4].wait()
    eye = hot(iota((32, 32), 0) == iota((32, 32), 1))

    def bases(p, carry):
        for w in range(2):
            bt[p, w] = dot_t(eye, basis_v[p, w]).astype(BF16)
            for q in range(2):
                i = 2 * w + q
                bp[p, :, 32 * i : 32 * i + 32] = dot(
                    permt[p], basis_v[p, w, PN * q : PN * q + PN]
                ).astype(BF16)
        return carry

    lax.fori_loop(0, 4, bases, 0)
    cbig[...] = jnp.zeros_like(cbig)

    offset = (h * HALF).astype(F32)
    for k in range(GM):
        if k:
            cb_out(k).wait_recv()
        row = cbr[k, 0:1, :] - offset
        here = slice(128 * k, 128 * k + 128)
        oht[:, here] = hot(iota((HALF, 128), 0) == row)
        col = columns(row)
        for t in range(HALF // 128):
            oh[here, 128 * t : 128 * t + 128] = hot(col == iota((128, 128), 1) + float(128 * t))

    for w4 in range(4):
        for b in range(2):
            halo_out(w4, b).wait_recv()
        far = dot(sel_r[...], hr1[w4]).astype(BF16)
        for p in range(4):
            u[p, w4, CORE + 64 : PN] = far[64 * p : 64 * p + 64]

    def gather(p, carry):
        for w in range(2):
            for q in range(2):
                gath[p, w, PN * q : PN * q + PN] = dot(perm[p], u[p, 2 * w + q]).astype(BF16)
            part = dot(bt[p, w], gath[p, w]).astype(BF16)
            for e in range(2):
                sb1[2 * w + e, pl.ds(32 * p, 32)] = part[:, 128 * e : 128 * e + 128]
        return carry

    lax.fori_loop(0, 4, gather, 0)

    def stage_a(k):
        mm = (m + k) % GM
        return remote(sb1.at[mm % XS], xb.at[pl.ds(128 * k, 128)], a_ss.at[k], a_rs.at[k], at_member(mm))

    for k in range(1, GM):
        stage_a(k).start()
    xb[0:128] = sb1[x]

    def local(i, carry):
        p, w = i // 2, i % 2
        inv_copy(i).wait()
        for q in range(2):
            loc = dot(inv_v[i, PN * q : PN * q + PN, :], gath[p, w]).astype(BF16)
            y = dot(permt[p], loc)
            own[2 * w + q, pl.ds(pl.multiple_of(CORE * p, CORE), CORE)] = y[0:CORE]
            yor[2 * w + q, p] = y[CORE:PN]
        return carry

    lax.fori_loop(0, 3, local, 0)

    for k in range(1, GM):
        stage_a(k).wait_recv()
    db[...] = dot(oht[...], xb[...]).astype(BF16)

    def stage_b(k):
        gg = (g + k) % groups
        return remote(
            db.at[pl.ds(pl.multiple_of(orow * gg, orow), orow)], s2.at[k],
            b_ss.at[k], b_rs.at[k], at_group(gg),
        )

    for k in range(1, groups):
        stage_b(k).start()

    lax.fori_loop(3, 6, local, 0)

    own_rows = pl.ds(pl.multiple_of(orow * g, orow), orow)
    total = db[own_rows].astype(F32)
    for k in range(1, groups):
        stage_b(k).wait_recv()
        total = total + s2[k].astype(F32)
    t_hi = total.astype(BF16)
    t_lo = (total - t_hi.astype(F32)).astype(BF16)

    @pl.when(x != holder)
    def _():
        ci_out(1).wait_recv()

    for b in range(per_owner):
        inv_b = ci_v[b, x // 2]
        rows = slice(32 * b, 32 * b + 32)
        cgs[rows] = (dot(inv_b, t_hi[rows]) + dot(inv_b, t_lo[rows])).astype(BF16)

    def stage_c(k):
        return remote(cgs, cg.at[own_rows], c_ss.at[k], c_rs.at[k], at_group((g + k) % groups))

    for k in range(1, groups):
        stage_c(k).start()
    cg[own_rows] = cgs[...]

    lax.fori_loop(6, 8, local, 0)

    for k in range(1, groups):
        stage_c(k).wait_recv()
    rb[...] = dot(oh[...], cg[...]).astype(BF16)

    def stage_d(k):
        return remote(
            rb.at[pl.ds(128 * k, 128)], cf.at[h, x], d_ss.at[k], d_rs.at[k],
            at_member((m + GM - k) % GM),
        )

    for k in range(1, GM):
        stage_d(k).start()
    cf[h, x] = rb[0:128]
    for k in range(1, GM):
        stage_d(k).wait_recv()

    for w in range(2):
        for e in range(2):
            both = cf[0, 2 * w + e] + cf[1, 2 * w + e]
            for p in range(4):
                for q in range(2):
                    i = 2 * w + q
                    cbig[p, 32 * i : 32 * i + 32, 256 * i + 128 * e : 256 * i + 128 * e + 128] = both[
                        32 * p : 32 * p + 32
                    ]
    for p in range(4):
        part = dot(bp[p, 448:512], cbig[p])
        for w4 in range(4):
            yr[w4, 64 * p : 64 * p + 64] = (
                yor[w4, p, 64:128] + part[:, 256 * w4 : 256 * w4 + 256]
            ).astype(BF16)

    def back(w4, b):
        return remote(
            hs2.at[w4, pl.ds(128 * b, 128)], hr2.at[w4, pl.ds(128 * b, 128)],
            hs2_sem.at[w4, b], hr2_sem.at[w4, b], lower if b == 0 else upper,
        )

    for w4 in range(4):
        hs2[w4] = dot(sel_rt[...], yr[w4]).astype(BF16)
        for b in range(2):
            back(w4, b).start()

    def coarse_own(p, carry):
        rows = pl.ds(pl.multiple_of(CORE * p, CORE), CORE)
        for w4 in range(4):
            part = dot(bp[p, 0:448], cbig[p, :, 256 * w4 : 256 * w4 + 256])
            own[w4, rows] += part[0:CORE]
            yo[w4, pl.ds(pl.multiple_of(64 * p, 64), 64)] = (
                yor[w4, p, 0:64] + part[CORE:448]
            ).astype(BF16)
        return carry

    lax.fori_loop(0, 4, coarse_own, 0)

    def spread(w4, carry):
        own[w4] += dot(sel_ot[...], yo[w4])
        return carry

    lax.fori_loop(0, 4, spread, 0)

    for w4 in range(4):
        for b in range(2):
            back(w4, b).wait_recv()
        out_ref[w4 // 2, w4 % 2] = (own[w4] + dot(sst[...], hr2[w4])).astype(BF16)

    for w4 in range(4):
        for b in range(2):
            halo_out(w4, b).wait_send()
            back(w4, b).wait_send()
    for k in range(1, GM):
        cb_out(k).wait_send()
        stage_a(k).wait_send()
        stage_d(k).wait_send()
    for k in range(1, groups):
        stage_b(k).wait_send()
        stage_c(k).wait_send()

    @pl.when(x == holder)
    def _():
        for k in range(1, XS):
            ci_out(k).wait_send()


def solution(mesh):
    groups = mesh.shape["patch"] // 2
    per_owner = 32 // groups
    vm = pltpu.VMEM
    dma = pltpu.SemaphoreType.DMA
    scratch = [
        vm((4, NODE, 256), BF16), vm((8, 1024, 1024), BF16), vm((4, 2, 1024, 32), BF16),
        vm((16, 2, 32, 32), BF16), vm((per_owner, 2, 32, 32), BF16),
        vm((4, 1, PN), F32),
        vm((256, NODE), BF16), vm((NODE, 256), BF16),
        vm((256, NODE), BF16), vm((NODE, 256), BF16),
        vm((256, 256), BF16), vm((256, 256), BF16),
        vm((4, PN, PN), BF16), vm((4, PN, PN), BF16),
        vm((4, 256, 256), BF16), vm((4, 256, 256), BF16),
        vm((4, 256, 256), BF16), vm((4, 256, 256), BF16),
        vm((4, 4, PN, 256), BF16), vm((4, 2, 1024, 256), BF16),
        vm((4, 2, 32, 1024), BF16), vm((4, PN, 128), BF16), vm((4, 128, 1024), BF16),
        vm((4, NODE, 256), F32), vm((4, 4, 128, 256), F32),
        vm((4, 256, 256), BF16), vm((4, 256, 256), BF16),
        vm((8, 128), F32), vm((GM, 8, 128), F32),
        vm((HALF, HALF), BF16), vm((HALF, HALF), BF16),
        vm((4, 128, 128), BF16), vm((HALF, 128), BF16), vm((HALF, 128), BF16),
        vm((groups, 32 * per_owner, 128), BF16), vm((32 * per_owner, 128), BF16),
        vm((HALF, 128), BF16), vm((HALF, 128), BF16), vm((2, 4, 128, 128), BF16),
        dma((6,)), dma((8,)), dma((4, 2)), dma((4, 2)), dma((4, 2)), dma((4, 2)),
        dma((GM,)), dma((GM,)), dma((XS,)), dma,
        dma((GM,)), dma((GM,)), dma((groups,)), dma((groups,)),
        dma((groups,)), dma((groups,)), dma((GM,)), dma((GM,)),
    ]

    def per_device(residual, patch_inv, coarse_basis, coarse_inv, patch_slots, send_rows, coarse_block):
        hbm = pl.BlockSpec(memory_space=pl.ANY)
        vmem = pl.BlockSpec(memory_space=pltpu.VMEM)
        return pl.pallas_call(
            functools.partial(kernel, groups),
            out_shape=jax.ShapeDtypeStruct(residual.shape, BF16),
            in_specs=[hbm, hbm, hbm, hbm, vmem, vmem, pl.BlockSpec(memory_space=pltpu.SMEM)],
            out_specs=vmem,
            scratch_shapes=scratch,
            compiler_params=pltpu.CompilerParams(
                collective_id=0, has_side_effects=True, vmem_limit_bytes=62 * 1024 * 1024
            ),
        )(residual, patch_inv, coarse_basis, coarse_inv, patch_slots, send_rows, coarse_block)

    node = P(None, None, ("patch", "coarse"), None)
    both = ("patch", "coarse")
    return jax.shard_map(
        per_device,
        mesh=mesh,
        in_specs=(
            node, P(both, None, None, None), P(both, None, None, None),
            P("coarse", None, None, None), P(both, None), P(both, None, None), P(both),
        ),
        out_specs=node,
        check_vma=False,
    )
```

time: 275 us -> 68.2 us (0.25)
  waiting for transfers between devices: 107 us -> 0 us
  matrix products: 84.7 us -> 0 us
  Pallas kernels: 0 us -> 60.8 us
  local copies, waits for them, and re-layouts: 42.4 us -> 6.38 us
  blocking collectives: 14.8 us -> 0 us
  between operations: 13.5 us -> 0.01 us
  starting transfers between devices: 12.3 us -> 0 us
    psum x1 -> x0, waiting for transfers between devices: 97.4 us -> none  [per_device(): totals = lax.psum(partial_sums, ('patch', 'coarse'))]
    dot_general x15 -> x0, matrix products: 84.7 us -> none  [the longest x3 23.4 us: spread_rows(): jnp.einsum(form, selector, upper_part, preferred_element_type=jnp.float32)]
    pallas_call x0 -> x1, Pallas kernels: none -> 60.8 us  [per_device(): pl.pallas_call(functools.partial(kernel, groups), out_shape=jax.ShapeDtyp...]
    reshape x2 -> x0, local copies, waits for them, and re-layouts: 28.4 us -> none  [the longest x1 28 us: per_device(): patch_inv.reshape(patches, wave_count, 2, patch_nodes, 2, patch_nodes)]
    all_gather x1 -> x0, blocking collectives: 14.8 us -> none  [per_device(): inverses = lax.all_gather(coarse_inv, 'coarse', axis=0, tiled=True)]
    ppermute x4 -> x0, starting transfers between devices: 12.3 us -> none  [passed_along(): return lax.ppermute(value, axis, pairs)]
    ppermute x4 -> x0, waiting for transfers between devices: 9.38 us -> none  [passed_along(): return lax.ppermute(value, axis, pairs)]
    convert_element_type x1 -> x0, local copies, waits for them, and re-layouts: 2.78 us -> none  [per_device(): return summed.astype(jnp.bfloat16)]
  transfers between devices with their start and end apart: 5 -> 0, of which waited for: 5 -> 0; matrix products, arithmetic and copies ran while one was open for 19% -> 0% of each run, Pallas kernels for 0% -> 0%
where the time goes in v1:
time: 68.2 us; the launch traced here: 67.2 us
  Pallas kernels  60.8 us (89%)
  local copies, waits for them, and re-layouts  6.38 us (9%)
    pallas_call x1, Pallas kernels, per_device(): pl.pallas_call(functools.partial(kernel, groups), out_shape=jax.ShapeDtyp...  60.8 us
    unnamed x2, local copies, waits for them, and re-layouts  6.38 us

profile of v1, /device:TPU:0, one launch (start us, length us, event | category | flops | bytes accessed | tf_op | source)
XLA Modules:
  0.0 67.2 jit_solution(562204963565425721)
XLA Ops:
  0.0 2.6 %copy.8.basis_hbm = bf16[4,2,1024,32]{3,2,1,0:T(8,128)(2,1)} copy(bf16[4,2,1024,32]{2,3,1,0:T(8,128)(2,1)} %param.9) | data formatting | bytes 1048576 | tf_op args[2]
  2.6 60.8 %shard_map.73 = bf16[2,2,1536,256]{3,2,1,0:T(8,128)(2,1)} custom-call(bf16[2,2,1536,256]{3,2,1,0:T(8,128)(2,1)} %res_hbm.1, bf16[4,2,1024,1024]{3,2,1,0:T(8,128)(2,1)} %inv_hbm.1, bf16[4,2,1024,32]{3,2,1,0:T(8,128)(2,1)} %copy.8.basis_hbm, bf16[16,2,32,32]{3,2,1,0:T(8,128)(2,1)} %cinv_hbm.1, s32[4,512]{1,0:T(4,128)} %slots_ref.1, s32[1,2,128]{2,1,0:T(2,128)} %send_ref.1, ...), custom_call_target="tpu_custom_call" | custom-call | tf_op jit(solution)/shard_map/pallas_call | solution.py:434
  63.4 3.8 %copy.10 = bf16[2,2,1536,256]{3,2,1,0:T(8,128)(2,1)} copy(bf16[2,2,1536,256]{3,2,1,0:T(8,128)(2,1)} %shard_map.73) | data formatting | bytes 6291456

commit v2 on v1

--- a/solution.py
+++ b/solution.py
@@ -44,7 +44,7 @@
     out_ref,
     res_v, inv_v, basis_v, cinv_v, ci_v,
     krow_s, ss, sst, sel_o, sel_ot, sel_r, sel_rt, perm, permt,
-    hs1, hr1, hs2, hr2, u, gath, bt, bp, cbig, own, yor, yo, yr,
+    hs1, hr1, hs2, hr2, u, gath, bp, cbig, own, yor, yo, yr,
     cbt, cbr, oh, oht, sb1, xb, db, s2, cgs, cg, rb, cf,
     load_sem, inv_sem, hs_sem, hr_sem, hs2_sem, hr2_sem,
     cb_ss, cb_rs, ci_ss, ci_rs, a_ss, a_rs, b_ss, b_rs, c_ss, c_rs, d_ss, d_rs,
@@ -78,7 +78,7 @@
         )
 
     loads = [
-        pltpu.make_async_copy(res_hbm.at[i // 2, i % 2], res_v.at[i], load_sem.at[i])
+        pltpu.make_async_copy(res_hbm.at[i // 2, i % 2], res_v.at[:, pl.ds(256 * i, 256)], load_sem.at[i])
         for i in range(4)
     ]
     loads.append(pltpu.make_async_copy(basis_hbm, basis_v, load_sem.at[4]))
@@ -88,9 +88,6 @@
 
     def inv_copy(i):
         return pltpu.make_async_copy(inv_hbm.at[i // 2, i % 2], inv_v.at[i], inv_sem.at[i])
-
-    for i in range(8):
-        inv_copy(i).start()
 
     barrier = pltpu.get_barrier_semaphore()
     peers = [upper, lower]
@@ -117,19 +114,22 @@
     cbt[...] = target.astype(F32)
     cbr[0] = target.astype(F32)
 
-    def halo_out(w4, b):
+    def halo_out(b):
         return remote(
-            hs1.at[w4, pl.ds(128 * b, 128)], hr1.at[w4, pl.ds(128 * b, 128)],
-            hs_sem.at[w4, b], hr_sem.at[w4, b], upper if b == 0 else lower,
-        )
-
-    for w4 in range(4):
-        loads[w4].wait()
-        hs1[w4] = dot(ss[...], res_v[w4]).astype(BF16)
-        if w4 == 0:
+            hs1.at[pl.ds(128 * b, 128)], hr1.at[pl.ds(128 * b, 128)],
+            hs_sem.at[b], hr_sem.at[b], upper if b == 0 else lower,
+        )
+
+    for i in range(4):
+        loads[i].wait()
+    for i in range(8):
+        inv_copy(i).start()
+    for b in range(2):
+        here = slice(128 * b, 128 * b + 128)
+        hs1[here] = dot(ss[here], res_v[...]).astype(BF16)
+        if b == 0:
             pl.semaphore_wait(barrier, len(peers))
-        for b in range(2):
-            halo_out(w4, b).start()
+        halo_out(b).start()
 
     def cb_out(k):
         return remote(cbt, cbr.at[k], cb_ss.at[k], cb_rs.at[k], at_member((m + k) % GM))
@@ -201,23 +201,18 @@
             )
         sel_rt[:, here] = hot(iota((256, 128), 0) == row_r)
 
-    for w4 in range(4):
-        others = dot(sel_o[...], res_v[w4]).astype(BF16)
-        for p in range(4):
-            u[p, w4, 0:CORE] = res_v[w4, CORE * p : CORE * p + CORE]
-            u[p, w4, CORE : CORE + 64] = others[64 * p : 64 * p + 64]
+    others = dot(sel_o[...], res_v[...]).astype(BF16)
+    for p in range(4):
+        u[p, 0:CORE] = res_v[CORE * p : CORE * p + CORE]
+        u[p, CORE : CORE + 64] = others[64 * p : 64 * p + 64]
 
     loads[4].wait()
-    eye = hot(iota((32, 32), 0) == iota((32, 32), 1))
 
     def bases(p, carry):
-        for w in range(2):
-            bt[p, w] = dot_t(eye, basis_v[p, w]).astype(BF16)
-            for q in range(2):
-                i = 2 * w + q
-                bp[p, :, 32 * i : 32 * i + 32] = dot(
-                    permt[p], basis_v[p, w, PN * q : PN * q + PN]
-                ).astype(BF16)
+        rows = jnp.concatenate(
+            [basis_v[p, i // 2, :, PN * (i % 2) : PN * (i % 2) + PN] for i in range(4)], axis=0
+        )
+        bp[p] = dot_t(permt[p], rows).astype(BF16)
         return carry
 
     lax.fori_loop(0, 4, bases, 0)
@@ -234,18 +229,18 @@
         for t in range(HALF // 128):
             oh[here, 128 * t : 128 * t + 128] = hot(col == iota((128, 128), 1) + float(128 * t))
 
-    for w4 in range(4):
-        for b in range(2):
-            halo_out(w4, b).wait_recv()
-        far = dot(sel_r[...], hr1[w4]).astype(BF16)
-        for p in range(4):
-            u[p, w4, CORE + 64 : PN] = far[64 * p : 64 * p + 64]
+    for b in range(2):
+        halo_out(b).wait_recv()
+    far = dot(sel_r[...], hr1[...]).astype(BF16)
+    for p in range(4):
+        u[p, CORE + 64 : PN] = far[64 * p : 64 * p + 64]
 
     def gather(p, carry):
+        rows = dot(perm[p], u[p]).astype(BF16)
+        for i in range(4):
+            gath[p, i // 2, PN * (i % 2) : PN * (i % 2) + PN] = rows[:, 256 * i : 256 * i + 256]
         for w in range(2):
-            for q in range(2):
-                gath[p, w, PN * q : PN * q + PN] = dot(perm[p], u[p, 2 * w + q]).astype(BF16)
-            part = dot(bt[p, w], gath[p, w]).astype(BF16)
+            part = dot(basis_v[p, w], gath[p, w]).astype(BF16)
             for e in range(2):
                 sb1[2 * w + e, pl.ds(32 * p, 32)] = part[:, 128 * e : 128 * e + 128]
         return carry
@@ -260,17 +255,19 @@
         stage_a(k).start()
     xb[0:128] = sb1[x]
 
-    def local(i, carry):
-        p, w = i // 2, i % 2
-        inv_copy(i).wait()
-        for q in range(2):
-            loc = dot(inv_v[i, PN * q : PN * q + PN, :], gath[p, w]).astype(BF16)
-            y = dot(permt[p], loc)
-            own[2 * w + q, pl.ds(pl.multiple_of(CORE * p, CORE), CORE)] = y[0:CORE]
-            yor[2 * w + q, p] = y[CORE:PN]
-        return carry
-
-    lax.fori_loop(0, 3, local, 0)
+    def local(p, carry):
+        for w in range(2):
+            inv_copy(2 * p + w).wait()
+            terms = dot(inv_v[2 * p + w], gath[p, w]).astype(BF16)
+            for q in range(2):
+                i = 2 * w + q
+                u[p, :, 256 * i : 256 * i + 256] = terms[PN * q : PN * q + PN]
+        y = dot(permt[p], u[p])
+        own[pl.ds(pl.multiple_of(CORE * p, CORE), CORE)] = y[0:CORE]
+        yor[p] = y[CORE:PN]
+        return carry
+
+    lax.fori_loop(0, 1, local, 0)
 
     for k in range(1, GM):
         stage_a(k).wait_recv()
@@ -286,7 +283,7 @@
     for k in range(1, groups):
         stage_b(k).start()
 
-    lax.fori_loop(3, 6, local, 0)
+    lax.fori_loop(1, 3, local, 0)
 
     own_rows = pl.ds(pl.multiple_of(orow * g, orow), orow)
     total = db[own_rows].astype(F32)
@@ -312,7 +309,7 @@
         stage_c(k).start()
     cg[own_rows] = cgs[...]
 
-    lax.fori_loop(6, 8, local, 0)
+    lax.fori_loop(3, 4, local, 0)
 
     for k in range(1, groups):
         stage_c(k).wait_recv()
@@ -341,49 +338,49 @@
                     ]
     for p in range(4):
         part = dot(bp[p, 448:512], cbig[p])
-        for w4 in range(4):
-            yr[w4, 64 * p : 64 * p + 64] = (
-                yor[w4, p, 64:128] + part[:, 256 * w4 : 256 * w4 + 256]
-            ).astype(BF16)
-
-    def back(w4, b):
+        yr[64 * p : 64 * p + 64] = (yor[p, 64:128] + part).astype(BF16)
+
+    def back(b):
         return remote(
-            hs2.at[w4, pl.ds(128 * b, 128)], hr2.at[w4, pl.ds(128 * b, 128)],
-            hs2_sem.at[w4, b], hr2_sem.at[w4, b], lower if b == 0 else upper,
-        )
-
-    for w4 in range(4):
-        hs2[w4] = dot(sel_rt[...], yr[w4]).astype(BF16)
-        for b in range(2):
-            back(w4, b).start()
+            hs2.at[pl.ds(128 * b, 128)], hr2.at[pl.ds(128 * b, 128)],
+            hs2_sem.at[b], hr2_sem.at[b], lower if b == 0 else upper,
+        )
+
+    hs2[...] = dot(sel_rt[...], yr[...]).astype(BF16)
+    for b in range(2):
+        back(b).start()
 
     def coarse_own(p, carry):
         rows = pl.ds(pl.multiple_of(CORE * p, CORE), CORE)
-        for w4 in range(4):
-            part = dot(bp[p, 0:448], cbig[p, :, 256 * w4 : 256 * w4 + 256])
-            own[w4, rows] += part[0:CORE]
-            yo[w4, pl.ds(pl.multiple_of(64 * p, 64), 64)] = (
-                yor[w4, p, 0:64] + part[CORE:448]
-            ).astype(BF16)
+        part = dot(bp[p, 0:448], cbig[p])
+        own[rows] += part[0:CORE]
+        yo[pl.ds(pl.multiple_of(64 * p, 64), 64)] = (yor[p, 0:64] + part[CORE:448]).astype(BF16)
         return carry
 
     lax.fori_loop(0, 4, coarse_own, 0)
 
-    def spread(w4, carry):
-        own[w4] += dot(sel_ot[...], yo[w4])
+    def spread(t, carry):
+        rows = pl.ds(pl.multiple_of(CORE * t, CORE), CORE)
+        own[rows] += dot(sel_ot[rows], yo[...])
         return carry
 
     lax.fori_loop(0, 4, spread, 0)
 
-    for w4 in range(4):
-        for b in range(2):
-            back(w4, b).wait_recv()
-        out_ref[w4 // 2, w4 % 2] = (own[w4] + dot(sst[...], hr2[w4])).astype(BF16)
-
-    for w4 in range(4):
-        for b in range(2):
-            halo_out(w4, b).wait_send()
-            back(w4, b).wait_send()
+    for b in range(2):
+        back(b).wait_recv()
+
+    def finish(t, carry):
+        rows = pl.ds(pl.multiple_of(CORE * t, CORE), CORE)
+        block = (own[rows] + dot(sst[rows], hr2[...])).astype(BF16)
+        for i in range(4):
+            out_ref[i // 2, i % 2, rows] = block[:, 256 * i : 256 * i + 256]
+        return carry
+
+    lax.fori_loop(0, 4, finish, 0)
+
+    for b in range(2):
+        halo_out(b).wait_send()
+        back(b).wait_send()
     for k in range(1, GM):
         cb_out(k).wait_send()
         stage_a(k).wait_send()
@@ -404,25 +401,25 @@
     vm = pltpu.VMEM
     dma = pltpu.SemaphoreType.DMA
     scratch = [
-        vm((4, NODE, 256), BF16), vm((8, 1024, 1024), BF16), vm((4, 2, 1024, 32), BF16),
+        vm((NODE, 1024), BF16), vm((8, 1024, 1024), BF16), vm((4, 2, 32, 1024), BF16),
         vm((16, 2, 32, 32), BF16), vm((per_owner, 2, 32, 32), BF16),
         vm((4, 1, PN), F32),
         vm((256, NODE), BF16), vm((NODE, 256), BF16),
         vm((256, NODE), BF16), vm((NODE, 256), BF16),
         vm((256, 256), BF16), vm((256, 256), BF16),
         vm((4, PN, PN), BF16), vm((4, PN, PN), BF16),
-        vm((4, 256, 256), BF16), vm((4, 256, 256), BF16),
-        vm((4, 256, 256), BF16), vm((4, 256, 256), BF16),
-        vm((4, 4, PN, 256), BF16), vm((4, 2, 1024, 256), BF16),
-        vm((4, 2, 32, 1024), BF16), vm((4, PN, 128), BF16), vm((4, 128, 1024), BF16),
-        vm((4, NODE, 256), F32), vm((4, 4, 128, 256), F32),
-        vm((4, 256, 256), BF16), vm((4, 256, 256), BF16),
+        vm((256, 1024), BF16), vm((256, 1024), BF16),
+        vm((256, 1024), BF16), vm((256, 1024), BF16),
+        vm((4, PN, 1024), BF16), vm((4, 2, 1024, 256), BF16),
+        vm((4, PN, 128), BF16), vm((4, 128, 1024), BF16),
+        vm((NODE, 1024), F32), vm((4, 128, 1024), F32),
+        vm((256, 1024), BF16), vm((256, 1024), BF16),
         vm((8, 128), F32), vm((GM, 8, 128), F32),
         vm((HALF, HALF), BF16), vm((HALF, HALF), BF16),
         vm((4, 128, 128), BF16), vm((HALF, 128), BF16), vm((HALF, 128), BF16),
         vm((groups, 32 * per_owner, 128), BF16), vm((32 * per_owner, 128), BF16),
         vm((HALF, 128), BF16), vm((HALF, 128), BF16), vm((2, 4, 128, 128), BF16),
-        dma((6,)), dma((8,)), dma((4, 2)), dma((4, 2)), dma((4, 2)), dma((4, 2)),
+        dma((6,)), dma((8,)), dma((2,)), dma((2,)), dma((2,)), dma((2,)),
         dma((GM,)), dma((GM,)), dma((XS,)), dma,
         dma((GM,)), dma((GM,)), dma((groups,)), dma((groups,)),
         dma((groups,)), dma((groups,)), dma((GM,)), dma((GM,)),
@@ -440,7 +437,7 @@
             compiler_params=pltpu.CompilerParams(
                 collective_id=0, has_side_effects=True, vmem_limit_bytes=62 * 1024 * 1024
             ),
-        )(residual, patch_inv, coarse_basis, coarse_inv, patch_slots, send_rows, coarse_block)
+        )(residual, patch_inv, jnp.swapaxes(coarse_basis, 2, 3), coarse_inv, patch_slots, send_rows, coarse_block)
 
     node = P(None, None, ("patch", "coarse"), None)
     both = ("patch", "coarse")

time: 68.2 us -> 65.1 us (0.955); the launches traced: 67.2 us -> 64.9 us
  local copies, waits for them, and re-layouts: 6.38 us -> 3.76 us
    unnamed x2 -> x1, local copies, waits for them, and re-layouts: 6.38 us -> 3.76 us
where the time goes in v2:
time: 65.1 us; the launch traced here: 64.9 us
  Pallas kernels  61.1 us (94%)
  local copies, waits for them, and re-layouts  3.76 us (6%)
    pallas_call x1, Pallas kernels, per_device(): pl.pallas_call(functools.partial(kernel, groups), out_shape=jax.ShapeDtyp...  61.1 us
    unnamed x1, local copies, waits for them, and re-layouts  3.76 us

profile of v2, /device:TPU:0, one launch (start us, length us, event | category | flops | bytes accessed | tf_op | source)
XLA Modules:
  0.0 64.9 jit_solution(13559511684528546192)
XLA Ops:
  0.0 61.1 %shard_map.73 = bf16[2,2,1536,256]{3,2,1,0:T(8,128)(2,1)} custom-call(bf16[2,2,1536,256]{3,2,1,0:T(8,128)(2,1)} %res_hbm.1, bf16[4,2,1024,1024]{3,2,1,0:T(8,128)(2,1)} %inv_hbm.1, bf16[4,2,32,1024]{3,2,1,0:T(8,128)(2,1)} %bitcast.1, bf16[16,2,32,32]{3,2,1,0:T(8,128)(2,1)} %cinv_hbm.1, s32[4,512]{1,0:T(4,128)} %slots_ref.1, s32[1,2,128]{2,1,0:T(2,128)} %send_ref.1, ...), custom_call_target="tpu_custom_call" | custom-call | tf_op jit(solution)/shard_map/pallas_call | solution.py:431
  61.2 3.8 %copy.9 = bf16[2,2,1536,256]{3,2,1,0:T(8,128)(2,1)} copy(bf16[2,2,1536,256]{3,2,1,0:T(8,128)(2,1)} %shard_map.73) | data formatting | bytes 6291456

commit v3 on v2

--- a/solution.py
+++ b/solution.py
@@ -41,9 +41,9 @@
 def kernel(
     groups,
     res_hbm, inv_hbm, basis_hbm, cinv_hbm, slots_ref, send_ref, cb_ref,
-    out_ref,
+    own_hbm, far_ref,
     res_v, inv_v, basis_v, cinv_v, ci_v,
-    krow_s, ss, sst, sel_o, sel_ot, sel_r, sel_rt, perm, permt,
+    krow_s, ss, sel_o, sel_ot, sel_r, sel_rt, perm, permt,
     hs1, hr1, hs2, hr2, u, gath, bp, cbig, own, yor, yo, yr,
     cbt, cbr, oh, oht, sb1, xb, db, s2, cgs, cg, rb, cf,
     load_sem, inv_sem, hs_sem, hr_sem, hs2_sem, hr2_sem,
@@ -103,7 +103,6 @@
             ss[128 * b : 128 * b + 128, 128 * t : 128 * t + 128] = hot(
                 col == iota((128, 128), 1) + float(128 * t)
             )
-        sst[:, 128 * b : 128 * b + 128] = hot(iota((NODE, 128), 0) == row)
 
     lane = lax.broadcasted_iota(jnp.int32, (8, 128), 1)
     target = jnp.where(
@@ -361,22 +360,24 @@
 
     def spread(t, carry):
         rows = pl.ds(pl.multiple_of(CORE * t, CORE), CORE)
-        own[rows] += dot(sel_ot[rows], yo[...])
+        res_v[rows] = (own[rows] + dot(sel_ot[rows], yo[...])).astype(BF16)
         return carry
 
     lax.fori_loop(0, 4, spread, 0)
 
+    stores = [
+        pltpu.make_async_copy(
+            res_v.at[:, pl.ds(256 * i, 256)], own_hbm.at[i // 2, i % 2], load_sem.at[i]
+        )
+        for i in range(4)
+    ]
+    for copy in stores:
+        copy.start()
     for b in range(2):
         back(b).wait_recv()
-
-    def finish(t, carry):
-        rows = pl.ds(pl.multiple_of(CORE * t, CORE), CORE)
-        block = (own[rows] + dot(sst[rows], hr2[...])).astype(BF16)
-        for i in range(4):
-            out_ref[i // 2, i % 2, rows] = block[:, 256 * i : 256 * i + 256]
-        return carry
-
-    lax.fori_loop(0, 4, finish, 0)
+    far_ref[...] = hr2[...]
+    for copy in stores:
+        copy.wait()
 
     for b in range(2):
         halo_out(b).wait_send()
@@ -393,6 +394,17 @@
     def _():
         for k in range(1, XS):
             ci_out(k).wait_send()
+
+
+def add_far(send_ref, own_ref, far_ref, out_ref):
+    rows = own_ref.shape[2]
+    ids = iota((rows, 128), 0) + (pl.program_id(0) * rows).astype(F32)
+    maps = [hot(ids == send_ref[0, b : b + 1, :].astype(F32)) for b in range(2)]
+    added = dot(jnp.concatenate(maps, axis=1), far_ref[...])
+    for i in range(4):
+        out_ref[i // 2, i % 2] = (
+            own_ref[i // 2, i % 2].astype(F32) + added[:, 256 * i : 256 * i + 256]
+        ).astype(BF16)
 
 
 def solution(mesh):
@@ -404,7 +416,7 @@
         vm((NODE, 1024), BF16), vm((8, 1024, 1024), BF16), vm((4, 2, 32, 1024), BF16),
         vm((16, 2, 32, 32), BF16), vm((per_owner, 2, 32, 32), BF16),
         vm((4, 1, PN), F32),
-        vm((256, NODE), BF16), vm((NODE, 256), BF16),
+        vm((256, NODE), BF16),
         vm((256, NODE), BF16), vm((NODE, 256), BF16),
         vm((256, 256), BF16), vm((256, 256), BF16),
         vm((4, PN, PN), BF16), vm((4, PN, PN), BF16),
@@ -428,16 +440,32 @@
     def per_device(residual, patch_inv, coarse_basis, coarse_inv, patch_slots, send_rows, coarse_block):
         hbm = pl.BlockSpec(memory_space=pl.ANY)
         vmem = pl.BlockSpec(memory_space=pltpu.VMEM)
-        return pl.pallas_call(
+        own, far = pl.pallas_call(
             functools.partial(kernel, groups),
-            out_shape=jax.ShapeDtypeStruct(residual.shape, BF16),
+            out_shape=(
+                jax.ShapeDtypeStruct(residual.shape, BF16),
+                jax.ShapeDtypeStruct((256, 1024), BF16),
+            ),
             in_specs=[hbm, hbm, hbm, hbm, vmem, vmem, pl.BlockSpec(memory_space=pltpu.SMEM)],
-            out_specs=vmem,
+            out_specs=(hbm, vmem),
             scratch_shapes=scratch,
             compiler_params=pltpu.CompilerParams(
                 collective_id=0, has_side_effects=True, vmem_limit_bytes=62 * 1024 * 1024
             ),
         )(residual, patch_inv, jnp.swapaxes(coarse_basis, 2, 3), coarse_inv, patch_slots, send_rows, coarse_block)
+        part = pl.BlockSpec((2, 2, CORE, 256), lambda t: (0, 0, t, 0))
+        return pl.pallas_call(
+            add_far,
+            grid=(NODE // CORE,),
+            out_shape=jax.ShapeDtypeStruct(residual.shape, BF16),
+            in_specs=[
+                pl.BlockSpec((1, 2, 128), lambda t: (0, 0, 0)),
+                part,
+                pl.BlockSpec((256, 1024), lambda t: (0, 0)),
+            ],
+            out_specs=part,
+            compiler_params=pltpu.CompilerParams(vmem_limit_bytes=32 * 1024 * 1024),
+        )(send_rows, own, far)
 
     node = P(None, None, ("patch", "coarse"), None)
     both = ("patch", "coarse")

time: 65.1 us -> 65.1 us (level)
  local copies, waits for them, and re-layouts: 3.76 us -> 2.93 us
  Pallas kernels: 61.1 us -> 61.9 us
    unnamed x1 -> x6, local copies, waits for them, and re-layouts: 3.76 us -> 2.93 us
    pallas_call x1 -> x2, Pallas kernels: 61.1 us -> 61.9 us  [the longest x1 58.8 us: per_device(): pl.pallas_call(functools.partial(kernel, groups), out_shape=(jax.ShapeDty...]
where the time goes in v3:
time: 65.1 us; the launch traced here: 64.8 us
  Pallas kernels  61.9 us (95%)
  local copies, waits for them, and re-layouts  2.93 us (5%)
    pallas_call x1, Pallas kernels, per_device(): pl.pallas_call(functools.partial(kernel, groups), out_shape=(jax.ShapeDty...  58.8 us
    pallas_call x1, Pallas kernels, per_device(): pl.pallas_call(add_far, grid=(NODE // CORE,), out_shape=jax.ShapeDtypeStr...  3.08 us
    unnamed x6, local copies, waits for them, and re-layouts  2.93 us

profile of v3, /device:TPU:0, one launch (start us, length us, event | category | flops | bytes accessed | tf_op | source)
XLA Modules:
  0.0 64.8 jit_solution(13291522463971843377)
XLA Ops:
  0.0 0.0 copy-start.2
  0.0 58.8 %shard_map.73 = (bf16[2,2,1536,256]{3,2,1,0:T(8,128)(2,1)}, bf16[256,1024]{1,0:T(8,128)(2,1)}) custom-call(bf16[2,2,1536,256]{3,2,1,0:T(8,128)(2,1)} %res_hbm.1, bf16[4,2,1024,1024]{3,2,1,0:T(8,128)(2,1)} %inv_hbm.1, bf16[4,2,32,1024]{3,2,1,0:T(8,128)(2,1)} %bitcast.1, bf16[16,2,32,32]{3,2,1,0:T(8,128)(2,1)} %cinv_hbm.1, s32[4,512]{1,0:T(4,128)} %slots_ref.1, ...), custom_call_target="tpu_custom_call" | custom-call | tf_op jit(solution)/shard_map/pallas_call | solution.py:443
  58.8 0.0 copy-done.2
  58.8 0.0 copy-start
  58.8 1.9 %copy-done = bf16[2,2,1536,256]{3,2,1,0:T(8,128)(2,1)S(1)} copy-done((bf16[2,2,1536,256]{3,2,1,0:T(8,128)(2,1)S(1)}, bf16[2,2,1536,256]{3,2,1,0:T(8,128)(2,1)}, u32[]{:S(2)}) %copy-start) | copy-done | bytes 3145752
  60.7 0.0 copy-start.1
  60.7 1.0 %copy-done.1 = bf16[256,1024]{1,0:T(8,128)(2,1)S(1)} copy-done((bf16[256,1024]{1,0:T(8,128)(2,1)S(1)}, bf16[256,1024]{1,0:T(8,128)(2,1)}, u32[]{:S(2)}) %copy-start.1) | copy-done | bytes 524312
  61.7 3.1 %shard_map.74 = bf16[2,2,1536,256]{3,2,1,0:T(8,128)(2,1)} custom-call(s32[1,2,128]{2,1,0:T(2,128)S(1)} %copy-done.2, bf16[2,2,1536,256]{3,2,1,0:T(8,128)(2,1)S(1)} %copy-done, bf16[256,1024]{1,0:T(8,128)(2,1)S(1)} %copy-done.1), custom_call_target="tpu_custom_call" | custom-call | tf_op jit(solution)/shard_map/pallas_call | solution.py:457
Async XLA Ops:
  0.0 58.8 %copy-start.2 = (s32[1,2,128]{2,1,0:T(2,128)S(1)}, s32[1,2,128]{2,1,0:T(2,128)}, u32[]{:S(2)}) copy-start(s32[1,2,128]{2,1,0:T(2,128)} %send_ref.3) | copy-start | bytes 3076
  58.8 1.9 %copy-start = (bf16[2,2,1536,256]{3,2,1,0:T(8,128)(2,1)S(1)}, bf16[2,2,1536,256]{3,2,1,0:T(8,128)(2,1)}, u32[]{:S(2)}) copy-start(bf16[2,2,1536,256]{3,2,1,0:T(8,128)(2,1)} %get-tuple-element.7.own_ref) | copy-start | bytes 9437188
  60.7 1.0 %copy-start.1 = (bf16[256,1024]{1,0:T(8,128)(2,1)S(1)}, bf16[256,1024]{1,0:T(8,128)(2,1)}, u32[]{:S(2)}) copy-start(bf16[256,1024]{1,0:T(8,128)(2,1)} %get-tuple-element.8.far_ref) | copy-start | bytes 1572868

commit v4 on v2

--- a/solution.py
+++ b/solution.py
@@ -44,7 +44,7 @@
     out_ref,
     res_v, inv_v, basis_v, cinv_v, ci_v,
     krow_s, ss, sst, sel_o, sel_ot, sel_r, sel_rt, perm, permt,
-    hs1, hr1, hs2, hr2, u, gath, bp, cbig, own, yor, yo, yr,
+    hs1, hr1, hs2, hr2, u, gath, bp, bpt, cbig, own, yor, yo, yr,
     cbt, cbr, oh, oht, sb1, xb, db, s2, cgs, cg, rb, cf,
     load_sem, inv_sem, hs_sem, hr_sem, hs2_sem, hr2_sem,
     cb_ss, cb_rs, ci_ss, ci_rs, a_ss, a_rs, b_ss, b_rs, c_ss, c_rs, d_ss, d_rs,
@@ -122,8 +122,6 @@
 
     for i in range(4):
         loads[i].wait()
-    for i in range(8):
-        inv_copy(i).start()
     for b in range(2):
         here = slice(128 * b, 128 * b + 128)
         hs1[here] = dot(ss[here], res_v[...]).astype(BF16)
@@ -213,6 +211,7 @@
             [basis_v[p, i // 2, :, PN * (i % 2) : PN * (i % 2) + PN] for i in range(4)], axis=0
         )
         bp[p] = dot_t(permt[p], rows).astype(BF16)
+        bpt[p] = dot(rows, perm[p]).astype(BF16)
         return carry
 
     lax.fori_loop(0, 4, bases, 0)
@@ -231,29 +230,39 @@
 
     for b in range(2):
         halo_out(b).wait_recv()
+    for i in range(8):
+        inv_copy(i).start()
     far = dot(sel_r[...], hr1[...]).astype(BF16)
     for p in range(4):
         u[p, CORE + 64 : PN] = far[64 * p : 64 * p + 64]
+
+    def restrict(p, carry):
+        full = dot(bpt[p], u[p])
+        for w in range(2):
+            part = full[64 * w : 64 * w + 32, 512 * w : 512 * w + 256]
+            part = part + full[64 * w + 32 : 64 * w + 64, 512 * w + 256 : 512 * w + 512]
+            part = part.astype(BF16)
+            for e in range(2):
+                sb1[2 * w + e, pl.ds(32 * p, 32)] = part[:, 128 * e : 128 * e + 128]
+        return carry
+
+    lax.fori_loop(0, 4, restrict, 0)
+
+    def stage_a(k):
+        mm = (m + k) % GM
+        return remote(sb1.at[mm % XS], xb.at[pl.ds(128 * k, 128)], a_ss.at[k], a_rs.at[k], at_member(mm))
+
+    for k in range(1, GM):
+        stage_a(k).start()
+    xb[0:128] = sb1[x]
 
     def gather(p, carry):
         rows = dot(perm[p], u[p]).astype(BF16)
         for i in range(4):
             gath[p, i // 2, PN * (i % 2) : PN * (i % 2) + PN] = rows[:, 256 * i : 256 * i + 256]
-        for w in range(2):
-            part = dot(basis_v[p, w], gath[p, w]).astype(BF16)
-            for e in range(2):
-                sb1[2 * w + e, pl.ds(32 * p, 32)] = part[:, 128 * e : 128 * e + 128]
         return carry
 
     lax.fori_loop(0, 4, gather, 0)
-
-    def stage_a(k):
-        mm = (m + k) % GM
-        return remote(sb1.at[mm % XS], xb.at[pl.ds(128 * k, 128)], a_ss.at[k], a_rs.at[k], at_member(mm))
-
-    for k in range(1, GM):
-        stage_a(k).start()
-    xb[0:128] = sb1[x]
 
     def local(p, carry):
         for w in range(2):
@@ -267,8 +276,6 @@
         yor[p] = y[CORE:PN]
         return carry
 
-    lax.fori_loop(0, 1, local, 0)
-
     for k in range(1, GM):
         stage_a(k).wait_recv()
     db[...] = dot(oht[...], xb[...]).astype(BF16)
@@ -283,7 +290,7 @@
     for k in range(1, groups):
         stage_b(k).start()
 
-    lax.fori_loop(1, 3, local, 0)
+    lax.fori_loop(0, 2, local, 0)
 
     own_rows = pl.ds(pl.multiple_of(orow * g, orow), orow)
     total = db[own_rows].astype(F32)
@@ -309,7 +316,7 @@
         stage_c(k).start()
     cg[own_rows] = cgs[...]
 
-    lax.fori_loop(3, 4, local, 0)
+    lax.fori_loop(2, 3, local, 0)
 
     for k in range(1, groups):
         stage_c(k).wait_recv()
@@ -324,6 +331,7 @@
     for k in range(1, GM):
         stage_d(k).start()
     cf[h, x] = rb[0:128]
+    lax.fori_loop(3, 4, local, 0)
     for k in range(1, GM):
         stage_d(k).wait_recv()
 
@@ -411,7 +419,7 @@
         vm((256, 1024), BF16), vm((256, 1024), BF16),
         vm((256, 1024), BF16), vm((256, 1024), BF16),
         vm((4, PN, 1024), BF16), vm((4, 2, 1024, 256), BF16),
-        vm((4, PN, 128), BF16), vm((4, 128, 1024), BF16),
+        vm((4, PN, 128), BF16), vm((4, 128, PN), BF16), vm((4, 128, 1024), BF16),
         vm((NODE, 1024), F32), vm((4, 128, 1024), F32),
         vm((256, 1024), BF16), vm((256, 1024), BF16),
         vm((8, 128), F32), vm((GM, 8, 128), F32),

time: 65.1 us -> 62.3 us (0.957)
  Pallas kernels: 61.1 us -> 58.3 us
    pallas_call x1, Pallas kernels: 61.1 us -> 58.3 us  [per_device(): pl.pallas_call(functools.partial(kernel, groups), out_shape=jax.ShapeDtyp...]
where the time goes in v4:
time: 62.3 us; the launch traced here: 62.1 us
  Pallas kernels  58.3 us (94%)
  local copies, waits for them, and re-layouts  3.76 us (6%)
    pallas_call x1, Pallas kernels, per_device(): pl.pallas_call(functools.partial(kernel, groups), out_shape=jax.ShapeDtyp...  58.3 us
    unnamed x1, local copies, waits for them, and re-layouts  3.76 us

profile of v4, /device:TPU:0, one launch (start us, length us, event | category | flops | bytes accessed | tf_op | source)
XLA Modules:
  0.0 62.1 jit_solution(13372623857922736954)
XLA Ops:
  0.0 58.3 %shard_map.73 = bf16[2,2,1536,256]{3,2,1,0:T(8,128)(2,1)} custom-call(bf16[2,2,1536,256]{3,2,1,0:T(8,128)(2,1)} %res_hbm.1, bf16[4,2,1024,1024]{3,2,1,0:T(8,128)(2,1)} %inv_hbm.1, bf16[4,2,32,1024]{3,2,1,0:T(8,128)(2,1)} %bitcast.1, bf16[16,2,32,32]{3,2,1,0:T(8,128)(2,1)} %cinv_hbm.1, s32[4,512]{1,0:T(4,128)} %slots_ref.1, s32[1,2,128]{2,1,0:T(2,128)} %send_ref.1, ...), custom_call_target="tpu_custom_call" | custom-call | tf_op jit(solution)/shard_map/pallas_call | solution.py:439
  58.3 3.8 %copy.9 = bf16[2,2,1536,256]{3,2,1,0:T(8,128)(2,1)} copy(bf16[2,2,1536,256]{3,2,1,0:T(8,128)(2,1)} %shard_map.73) | data formatting | bytes 6291456
